TPU v7x, 1024 devices: a whole 4x4x32 slice. The times are simulated.
1024 devices in a mesh: grp: 16 (over x, z_hi), inner: 64 (over y, z_lo, core).
Axes of the slice: x: 4, y: 4, z: 32 (z_hi: 4, z_lo: 8; z = z_hi * 8 + z_lo), core: 2. Of those that a mesh axis runs over, the one named last changes fastest.
Arguments:
- tokens: bfloat16 [131072, 4096], P(('grp', 'inner')), may hold values from -24 to 24
- norm_gain: float32 [4096], replicated, may hold values from 0.1 to 1.9
- key_weight: bfloat16 [4096, 512], P('inner'), may hold values from -0.09375 to 0.09375
- key_grad: bfloat16 [131072, 512], P(('grp', 'inner')), may hold values from -6 to 6
Outputs:
- keys: bfloat16 [131072, 512], P(('grp', 'inner'))
- input_grad: bfloat16 [131072, 4096], P(('grp', 'inner'))
- weight_grad: float32 [4096, 512], P(('grp', 'inner'))
All inputs are finite; a program needn't handle non-finite values.
Results may differ from a plain program's by a relative error of at most 0.015.
Values may be sent and summed in bfloat16 or wider, within the bound.
A program may use at most 64 MiB of HBM per device.

v0:
```python
import jax
import jax.numpy as jnp
from jax import lax
from jax.sharding import PartitionSpec as P

TOK_DEV = 128


def shards(tokens, norm_gain, key_weight, key_grad):
    gathered = lax.all_gather(key_weight, "inner", axis=0, tiled=True)
    values = tokens.astype(jnp.float32)
    inverse = lax.rsqrt(jnp.mean(values * values, axis=-1, keepdims=True) + 1e-05)
    unit = values * inverse
    normed = (unit * norm_gain).astype(jnp.bfloat16)
    keys = jnp.dot(normed, gathered, preferred_element_type=jnp.float32).astype(jnp.bfloat16)
    normed_grad = lax.dot_general(
        key_grad, gathered, (((1,), (1,)), ((), ())), preferred_element_type=jnp.float32
    )
    scaled_grad = normed_grad * norm_gain
    centre = jnp.mean(scaled_grad * unit, axis=-1, keepdims=True)
    input_grad = ((scaled_grad - unit * centre) * inverse).astype(jnp.bfloat16)
    groups = lax.axis_size("grp")
    members = lax.axis_size("inner")
    scale = (TOK_DEV * groups * members) ** (-0.5)
    term = lax.dot_general(
        normed, key_grad, (((0,), (0,)), ((), ())), preferred_element_type=jnp.float32
    )
    group_sum = lax.psum_scatter(
        term.astype(jnp.bfloat16), "grp", scatter_dimension=0, tiled=True
    ).astype(jnp.float32)
    weight_grad = lax.psum_scatter(group_sum, "inner", scatter_dimension=0, tiled=True) * scale
    return (keys, input_grad, weight_grad)


def solution(mesh):
    return jax.shard_map(
        shards,
        mesh=mesh,
        in_specs=(P(("grp", "inner"), None), P(), P("inner", None), P(("grp", "inner"), None)),
        out_specs=(P(("grp", "inner"), None), P(("grp", "inner"), None), P(("grp", "inner"), None)),
        check_vma=False,
    )
```

profile of v0, /device:TPU:1, one launch (start us, length us, event | category | flops | bytes accessed | tf_op | source)
XLA Modules:
  0.0 717.2 jit_solution(1733586476006908761)
XLA Ops:
  8.0 0.0 copy-start
  8.0 0.0 copy-start.1
  8.0 0.0 all-gather.2.cloned.1.call-start
  8.1 0.7 all-gather.2.cloned.1.call-update
  8.8 0.0 reduce-scatter.2.cloned.1.call-start
  8.8 1.5 fusion.8
  10.3 0.0 copy-done
  10.3 0.0 copy-done.1
  10.4 4.1 convolution_convert_fusion
  14.4 0.0 copy-start.3
  14.4 0.0 reduce-scatter.2.cloned.1.call-update
  14.4 1.3 dynamic-slice
  16.4 217.2 %all-gather.2.cloned.1.call-done = bf16[4096,512]{1,0:T(8,128)(2,1)} async-done(((bf16[64,512]{1,0:T(8,128)(2,1)}), bf16[4096,512]{1,0:T(8,128)(2,1)}) %all-gather.2.cloned.1.call-update) | async-done | bytes 4194320 | tf_op jit(solution)/shard_map/all_gather | solution.py:10
  233.6 0.0 copy-done.3
  233.6 0.0 copy-start.2
  233.6 3.9 fusion.4
  237.5 0.0 copy-done.2
  237.5 1.4 convolution_convert_fusion.1
  238.9 1.5 fusion.7
  240.4 54.5 %reduce-scatter.2.cloned.1.call-done = bf16[256,512]{1,0:T(8,128)(2,1)} async-done(((bf16[4096,512]{1,0:T(8,128)(2,1)}), bf16[256,512]{1,0:T(8,128)(2,1)}) %reduce-scatter.2.cloned.1.call-update) | async-done | bytes 262160 | tf_op jit(solution)/shard_map/reduce_scatter | solution.py:28
  294.9 414.2 %all-reduce.2 = f32[256,512]{1,0:T(8,128)S(1)} all-reduce(bf16[256,512]{1,0:T(8,128)(2,1)} %reduce-scatter.2.cloned.1.call-done), channel_id=3, replica_groups=mesh['grp'=16,'inner'=64] {'inner'}, use_global_device_ids=true, to_apply=%region_3.0.clone | all-reduce | flops 131072 | bytes 786432
  709.1 0.6 dynamic-slice_multiply_fusion
  (2 shorter events, 0.0 us)
Async XLA Ops:
  8.0 2.3 copy-start
  8.0 2.3 copy-start.1
  8.0 225.6 %all-gather.2.cloned.1.call-start = ((), (), s32[]{:S(2)}) async-start(), calls=%async_computation.1 | async-start | bytes 4259840 | tf_op jit(solution)/shard_map/all_gather | solution.py:10
  8.8 286.1 %reduce-scatter.2.cloned.1.call-start = ((), (), s32[]{:S(2)}) async-start(), calls=%async_computation.2 | async-start | bytes 4456448 | tf_op jit(solution)/shard_map/reduce_scatter | solution.py:28
  14.4 219.2 %copy-start.3 = (f32[4096]{0:T(1024)S(1)}, f32[4096]{0:T(1024)}, u32[]{:S(2)}) copy-start(f32[4096]{0:T(1024)} %param.5) | copy-start | bytes 49156
  233.6 3.9 copy-start.2
Sparse Core Ops, SparseCore 0:
  11.6 221.9 all-gather.1
Sparse Core Ops, SparseCore 1:
  14.6 280.2 reduce-scatter.1
where the time goes:
time: 726 us; the launch traced here: 717 us
  blocking collectives  414 us (57%)
  waiting for transfers between devices  272 us (37%)
  between operations  16.2 us (2%)
  matrix products  9.39 us (1%)
    unnamed x1, blocking collectives  414 us
    all_gather x1, waiting for transfers between devices, shards(): gathered = lax.all_gather(key_weight, 'inner', axis=0, tiled=True)  217 us
    reduce_scatter x1, waiting for transfers between devices, shards(): lax.psum_scatter(term.astype(jnp.bfloat16), 'grp', scatter_dimension=0, t...  54.5 us
  transfers between devices with their start and end apart: 2, of which 2 were waited for; matrix products, arithmetic and copies ran while one was open for 2% of the time, Pallas kernels for 0%

commit v1 on v0

v1 whole, which is shorter than its diff:
```python
import functools

import jax
import jax.numpy as jnp
from jax import lax
from jax.experimental import pallas as pl
from jax.experimental.pallas import tpu as pltpu
from jax.sharding import PartitionSpec as P

TOK = 128
D = 4096
KW = 512
TOKENS = 131072
F32 = jnp.float32
BF16 = jnp.bfloat16
MESH = pl.DeviceIdType.MESH
WINDOW = (-4, -3, -2, -1, 1, 2, 3)
Z_PEERS = (1, 2, 3, 4, 8, 12, 16, 20, 24, 28, 29, 30, 31)


def kernel(
    tok_ref, gain_ref, w_ref, kg_ref, keys_ref, ig_ref, wg_ref,
    n2, kg2, inv, ta, tb, ra, rb, sa, sb, ra2, rb2, zbuf, rza, zb2, rzb,
    fsend, frecv, wbuf, sg, acc,
    swap_s, swap_r, gz_s, gz_r, a1_s, a1_r, b1_s, b1_r, a2_s, a2_r, b2_s, b2_r,
    za_s, za_r, zb_s, zb_r, g0p_s, g0p_r, g1p_s, g1p_r, g0q_s, g0q_r, g1q_s, g1q_r,
    fw_s, fw_r, fin_s, fin_r,
):
    grp = lax.axis_index("grp")
    inner = lax.axis_index("inner")
    x = grp // 4
    z = (grp % 4) * 8 + (inner // 2) % 8
    y = inner // 16
    c = inner % 2
    oc = 1 - c
    zl = z % 8
    zg = z // 4
    zm = z % 4

    def dev(px, py, pz, pc):
        return (px * 4 + pz // 8, (py * 8 + pz % 8) * 2 + pc)

    sends = []

    def send(src, dst, s, r, target):
        copy = pltpu.make_async_remote_copy(
            src_ref=src, dst_ref=dst, send_sem=s, recv_sem=r,
            device_id=target, device_id_type=MESH,
        )
        copy.start()
        sends.append(copy)
        return copy

    xp = [(x + k) % 4 for k in range(4)]
    yp = [(y + k) % 4 for k in range(4)]
    partner = dev(x, y, z, oc)

    barrier = pltpu.get_barrier_semaphore()
    peers = [partner]
    peers += [dev(xp[k], y, z, c) for k in (1, 2, 3)]
    peers += [dev(x, yp[k], z, c) for k in (1, 2, 3)]
    peers += [dev(x, y, (z + k) % 32, c) for k in Z_PEERS]
    for peer in peers:
        pl.semaphore_signal(barrier, inc=1, device_id=peer, device_id_type=MESH)

    total = jnp.zeros((TOK, 128), F32)
    for j in range(D // 512):
        v = tok_ref[:, j * 512:(j + 1) * 512].astype(F32)
        v = v * v
        for i in range(4):
            total = total + v[:, i * 128:(i + 1) * 128]
    inverse = lax.rsqrt(jnp.sum(total, axis=-1, keepdims=True) * (1.0 / D) + 1e-05)
    inv[...] = inverse
    for j in range(4):
        v = tok_ref[:, j * 1024:(j + 1) * 1024].astype(F32) * inverse
        n2[c, j] = (v * gain_ref[:, j * 1024:(j + 1) * 1024]).astype(BF16)
    kg2[c] = kg_ref[:, pl.ds(pl.multiple_of(c * 256, 256), 256)]
    wbuf[y, zl, c * 4 + x] = w_ref[pl.ds(pl.multiple_of(x * 16, 16), 16), :]

    pl.semaphore_wait(barrier, len(peers))

    kg_copy = send(
        kg_ref.at[:, pl.ds(pl.multiple_of(oc * 256, 256), 256)], kg2.at[c],
        swap_s.at[4], swap_r.at[4], partner,
    )
    order = (2, 1, 3, 0)
    swaps = {}
    for k in order:
        swaps[k] = send(n2.at[c, xp[k]], n2.at[c, xp[k]], swap_s.at[k], swap_r.at[k], partner)

    gz = []
    for n, k in enumerate(WINDOW):
        piece = wbuf.at[y, zl, c * 4 + x]
        gz.append(send(piece, piece, gz_s.at[n], gz_r.at[n], dev(x, y, (z + k) % 32, c)))

    kg_copy.wait_recv()
    a1, b1 = {}, {}
    for k in order:
        swaps[k].wait_recv()
        xt = xp[k]
        for j in range(4):
            lhs = n2[:, xt, :, j * 256:(j + 1) * 256].reshape(2 * TOK, 256)
            t = lax.dot_general(
                lhs, kg2[...].reshape(2 * TOK, 256), (((0,), (0,)), ((), ())),
                preferred_element_type=F32,
            ).astype(BF16)
            ta[xt, j] = t[:, :128].reshape(4, 64, 128)
            tb[xt, j] = t[:, 128:].reshape(4, 64, 128)
        if k:
            a1[k] = send(ta.at[xt], ra.at[k - 1], a1_s.at[k - 1], a1_r.at[k - 1], dev(xt, y, z, c))
    for k in (2, 1, 3):
        b1[k] = send(
            tb.at[:, :, yp[k]], rb.at[k - 1], b1_s.at[k - 1], b1_r.at[k - 1], dev(x, yp[k], z, c)
        )

    for copy in gz:
        copy.wait_recv()

    for k in (1, 3, 2):
        a1[k].wait_recv()
    for j in range(4):
        v = ta[x, j].astype(F32)
        for k in range(3):
            v = v + ra[k, j].astype(F32)
        sa[j] = v.astype(BF16)
    a2 = [
        send(sa.at[:, yp[k]], ra2.at[k - 1], a2_s.at[k - 1], a2_r.at[k - 1], dev(x, yp[k], z, c))
        for k in (2, 1, 3)
    ]
    for k in (1, 3, 2):
        b1[k].wait_recv()
    for j in range(4):
        v = tb[j, :, y].astype(F32)
        for k in range(3):
            v = v + rb[k, j].astype(F32)
        sb[j] = v.astype(BF16)
    b2 = [
        send(sb.at[xp[k]], rb2.at[k - 1], b2_s.at[k - 1], b2_r.at[k - 1], dev(xp[k], y, z, c))
        for k in (2, 1, 3)
    ]
    g0p = []
    g1p = []
    for k in (2, 1, 3):
        piece = wbuf.at[y, 0:4, c * 4 + x]
        g0p.append(send(piece, piece, g0p_s.at[k - 1], g0p_r.at[k - 1], dev(xp[k], y, z, c)))
        piece = wbuf.at[y, 4:8, c * 4 + x]
        g1p.append(send(piece, piece, g1p_s.at[k - 1], g1p_r.at[k - 1], dev(x, yp[k], z, c)))

    for copy in a2:
        copy.wait_recv()
    for copy in b2:
        copy.wait_recv()
    fa = sa[:, y].astype(F32)
    fb = sb[x].astype(F32)
    for k in range(3):
        fa = fa + ra2[k].astype(F32)
        fb = fb + rb2[k].astype(F32)
    both = jnp.concatenate([fa.reshape(8, 4, 8, 128), fb.reshape(8, 4, 8, 128)], axis=2)
    zbuf[...] = both.astype(BF16)
    za = [
        send(
            zbuf.at[:, (zm + k) % 4], rza.at[k - 1], za_s.at[k - 1], za_r.at[k - 1],
            dev(x, y, zg * 4 + (zm + k) % 4, c),
        )
        for k in (1, 2, 3)
    ]

    forwards = []

    def forward(piece):
        n = len(forwards)
        forwards.append(send(piece, piece, fw_s.at[n], fw_r.at[n], partner))

    for copy in g0p:
        copy.wait_recv()
    g0q = {}
    for k in (2, 1, 3):
        piece = wbuf.at[y, 0:4, pl.ds(c * 4, 4)]
        g0q[k] = send(piece, piece, g0q_s.at[k - 1], g0q_r.at[k - 1], dev(x, yp[k], z, c))
    for copy in g1p:
        copy.wait_recv()
    g1q = {}
    for k in (2, 1, 3):
        piece = wbuf.at[:, 4:8, c * 4 + x]
        g1q[k] = send(piece, piece, g1q_s.at[k - 1], g1q_r.at[k - 1], dev(xp[k], y, z, c))
    forward(wbuf.at[y, 0:4, pl.ds(c * 4, 4)])
    forward(wbuf.at[:, 4:8, c * 4 + x])

    for copy in za:
        copy.wait_recv()
    v = zbuf[:, zm].astype(F32)
    for k in range(3):
        v = v + rza[k].astype(F32)
    zb2[...] = v.astype(BF16)
    zb = []
    for k in (4, 3, 5, 2, 6, 1, 7):
        gt = (zg + k) % 8
        zb.append(
            send(zb2.at[gt], rzb.at[k - 1], zb_s.at[k - 1], zb_r.at[k - 1], dev(x, y, gt * 4 + zm, c))
        )

    for k in (1, 3, 2):
        g0q[k].wait_recv()
        forward(wbuf.at[yp[4 - k], 0:4, pl.ds(c * 4, 4)])
        g1q[k].wait_recv()
        forward(wbuf.at[:, 4:8, c * 4 + xp[4 - k]])

    for copy in zb:
        copy.wait_recv()
    v = zb2[zg].astype(F32)
    for k in range(7):
        v = v + rzb[k].astype(F32)
    v = v * (TOKENS ** -0.5)
    low = jnp.concatenate([v[0:4], v[8:12]], axis=0)
    high = jnp.concatenate([v[4:8], v[12:16]], axis=0)
    mine = jnp.where(c == 0, low, high)
    fsend[...] = jnp.where(c == 0, high, low)
    fin = send(fsend, frecv, fin_s.at[0], fin_r.at[0], partner)

    for copy in forwards:
        copy.wait_recv()
    acc[...] = jnp.zeros_like(acc)

    def block(j, dots):
        for i in range(4):
            rows = slice(i * 256, (i + 1) * 256)
            w = wbuf[j, i * 2:(i + 1) * 2].reshape(256, KW)
            normed = n2[c, j, :, rows]
            acc[...] += jnp.dot(normed, w, preferred_element_type=F32)
            cols = pl.ds(pl.multiple_of(j * 1024 + i * 256, 256), 256)
            ng = lax.dot_general(
                kg_ref[...], w, (((1,), (1,)), ((), ())), preferred_element_type=F32
            )
            s = ng * gain_ref[:, cols]
            sg[j, :, rows] = s
            p = s * (tok_ref[:, cols].astype(F32) * inv[...])
            dots = dots + p[:, :128] + p[:, 128:]
        return dots

    dots = lax.fori_loop(0, 4, block, jnp.zeros((TOK, 128), F32))
    keys_ref[...] = acc[...].astype(BF16)
    centre = jnp.sum(dots, axis=-1, keepdims=True) * (1.0 / D)

    def finish(j, carry):
        cols = pl.ds(pl.multiple_of(j * 1024, 1024), 1024)
        unit = tok_ref[:, cols].astype(F32) * inv[...]
        ig_ref[:, cols] = ((sg[j] - unit * centre) * inv[...]).astype(BF16)
        return carry

    lax.fori_loop(0, 4, finish, 0)

    fin.wait_recv()
    other = frecv[...]
    first = jnp.where(c == 0, mine, other)
    second = jnp.where(c == 0, other, mine)
    wg_ref[:, 0:128] = first[0:4]
    wg_ref[:, 128:256] = first[4:8]
    wg_ref[:, 256:384] = second[0:4]
    wg_ref[:, 384:512] = second[4:8]

    for copy in sends:
        copy.wait_send()


def shards(tokens, norm_gain, key_weight, key_grad):
    vmem = pl.BlockSpec(memory_space=pltpu.VMEM)
    pairs = (5, 7, 3, 3, 3, 3, 3, 7, 3, 3, 3, 3, 8, 1)
    sems = []
    for n in pairs:
        sems += [pltpu.SemaphoreType.DMA((n,)), pltpu.SemaphoreType.DMA((n,))]
    return pl.pallas_call(
        kernel,
        name="key_projection",
        out_shape=(
            jax.ShapeDtypeStruct((TOK, KW), BF16),
            jax.ShapeDtypeStruct((TOK, D), BF16),
            jax.ShapeDtypeStruct((4, KW), F32),
        ),
        in_specs=[vmem] * 4,
        out_specs=(vmem, vmem, vmem),
        scratch_shapes=[
            pltpu.VMEM((2, 4, TOK, 1024), BF16),
            pltpu.VMEM((2, TOK, 256), BF16),
            pltpu.VMEM((TOK, 1), F32),
            pltpu.VMEM((4, 4, 4, 64, 128), BF16),
            pltpu.VMEM((4, 4, 4, 64, 128), BF16),
            pltpu.VMEM((3, 4, 4, 64, 128), BF16),
            pltpu.VMEM((3, 4, 4, 64, 128), BF16),
            pltpu.VMEM((4, 4, 64, 128), BF16),
            pltpu.VMEM((4, 4, 64, 128), BF16),
            pltpu.VMEM((3, 4, 64, 128), BF16),
            pltpu.VMEM((3, 4, 64, 128), BF16),
            pltpu.VMEM((8, 4, 16, 128), BF16),
            pltpu.VMEM((3, 8, 16, 128), BF16),
            pltpu.VMEM((8, 16, 128), BF16),
            pltpu.VMEM((7, 16, 128), BF16),
            pltpu.VMEM((8, 128), F32),
            pltpu.VMEM((8, 128), F32),
            pltpu.VMEM((4, 8, 8, 16, KW), BF16),
            pltpu.VMEM((4, TOK, 1024), F32),
            pltpu.VMEM((TOK, KW), F32),
        ] + sems,
        compiler_params=pltpu.CompilerParams(
            collective_id=0, has_side_effects=True, vmem_limit_bytes=48 * 2**20
        ),
    )(tokens, norm_gain.reshape(1, D), key_weight, key_grad)


def solution(mesh):
    return jax.shard_map(
        shards,
        mesh=mesh,
        in_specs=(P(("grp", "inner"), None), P(), P("inner", None), P(("grp", "inner"), None)),
        out_specs=(P(("grp", "inner"), None), P(("grp", "inner"), None), P(("grp", "inner"), None)),
        check_vma=False,
    )
```

time: 726 us -> 83.6 us (0.12); the launches traced: 717 us -> 83.3 us
  blocking collectives: 414 us -> 0 us
  waiting for transfers between devices: 272 us -> 0 us
  Pallas kernels: 0 us -> 76.7 us
  between operations: 16.2 us -> 0.65 us
  matrix products: 9.39 us -> 0 us
    unnamed x1 -> x0, blocking collectives: 414 us -> none
    all_gather x1 -> x0, waiting for transfers between devices: 217 us -> none  [shards(): gathered = lax.all_gather(key_weight, 'inner', axis=0, tiled=True)]
    pallas_call x0 -> x1, Pallas kernels: none -> 76.7 us  [shards(): pl.pallas_call(kernel, name='key_projection', out_shape=(jax.ShapeDtypeSt...]
    reduce_scatter x1 -> x0, waiting for transfers between devices: 54.5 us -> none  [shards(): lax.psum_scatter(term.astype(jnp.bfloat16), 'grp', scatter_dimension=0, t...]
    dot_general x3 -> x0, matrix products: 9.39 us -> none  [the longest x1 4.06 us: shards(): lax.dot_general(normed, key_grad, (((0,), (0,)), ((), ())), preferred_ele...]
  transfers between devices with their start and end apart: 2 -> 0, of which waited for: 2 -> 0; matrix products, arithmetic and copies ran while one was open for 2% -> 0% of each run, Pallas kernels for 0% -> 0%
where the time goes in v1:
time: 83.6 us; the launch traced here: 83.3 us
  Pallas kernels  76.7 us (92%)
  local copies, waits for them, and re-layouts  5.9 us (7%)
    pallas_call x1, Pallas kernels, shards(): pl.pallas_call(kernel, name='key_projection', out_shape=(jax.ShapeDtypeSt...  76.7 us
    unnamed x11, local copies, waits for them, and re-layouts  5.9 us

profile of v1, /device:TPU:1, one launch (start us, length us, event | category | flops | bytes accessed | tf_op | source)
XLA Modules:
  0.0 83.3 jit_solution(8881054307193155989)
XLA Ops:
  0.6 0.0 copy-start
  0.6 1.2 %copy-done = bf16[128,4096]{1,0:T(8,128)(2,1)S(1)} copy-done((bf16[128,4096]{1,0:T(8,128)(2,1)S(1)}, bf16[128,4096]{1,0:T(8,128)(2,1)}, u32[]{:S(2)}) %copy-start) | copy-done | bytes 1048600
  1.9 0.0 copy-start.1
  1.9 0.9 %copy-done.1 = bf16[128,512]{1,0:T(8,128)(2,1)S(1)} copy-done((bf16[128,512]{1,0:T(8,128)(2,1)S(1)}, bf16[128,512]{1,0:T(8,128)(2,1)}, u32[]{:S(2)}) %copy-start.1) | copy-done | bytes 131096
  2.8 0.0 copy-start.2
  2.8 0.8 %copy-done.2 = bf16[64,512]{1,0:T(8,128)(2,1)S(1)} copy-done((bf16[64,512]{1,0:T(8,128)(2,1)S(1)}, bf16[64,512]{1,0:T(8,128)(2,1)}, u32[]{:S(2)}) %copy-start.2) | copy-done | bytes 65560
  3.6 0.0 copy-start.3
  3.6 0.7 copy-done.3
  4.3 76.7 %key_projection.1 = (bf16[128,512]{1,0:T(8,128)(2,1)S(1)}, bf16[128,4096]{1,0:T(8,128)(2,1)S(1)}, f32[4,512]{1,0:T(4,128)S(1)}) custom-call(bf16[128,4096]{1,0:T(8,128)(2,1)S(1)} %copy-done, f32[1,4096]{1,0:T(1,128)S(1)} %bitcast.1, bf16[64,512]{1,0:T(8,128)(2,1)S(1)} %copy-done.2, bf16[128,512]{1,0:T(8,128)(2,1)S(1)} %copy-done.1), custom_call_target="tpu_custom_call" | custom-call | tf_op jit(solution)/shard_map/key_projection/pallas_call | solution.py:271
  81.0 0.7 copy.10
  81.7 1.0 %copy.11 = bf16[128,4096]{1,0:T(8,128)(2,1)} copy(bf16[128,4096]{1,0:T(8,128)(2,1)S(1)} %get-tuple-element.7) | data formatting | bytes 2097152
  82.7 0.6 copy.12
Async XLA Ops:
  0.6 1.2 %copy-start = (bf16[128,4096]{1,0:T(8,128)(2,1)S(1)}, bf16[128,4096]{1,0:T(8,128)(2,1)}, u32[]{:S(2)}) copy-start(bf16[128,4096]{1,0:T(8,128)(2,1)} %tok_ref.1) | copy-start | bytes 3145732
  1.9 0.9 %copy-start.1 = (bf16[128,512]{1,0:T(8,128)(2,1)S(1)}, bf16[128,512]{1,0:T(8,128)(2,1)}, u32[]{:S(2)}) copy-start(bf16[128,512]{1,0:T(8,128)(2,1)} %kg_ref.1) | copy-start | bytes 393220
  2.8 0.8 %copy-start.2 = (bf16[64,512]{1,0:T(8,128)(2,1)S(1)}, bf16[64,512]{1,0:T(8,128)(2,1)}, u32[]{:S(2)}) copy-start(bf16[64,512]{1,0:T(8,128)(2,1)} %w_ref.1) | copy-start | bytes 196612
  3.6 0.7 copy-start.3

commit v2 on v1

v2 whole, which is shorter than its diff:
```python
import functools

import jax
import jax.numpy as jnp
from jax import lax
from jax.experimental import pallas as pl
from jax.experimental.pallas import tpu as pltpu
from jax.sharding import PartitionSpec as P

TOK = 128
D = 4096
KW = 512
TOKENS = 131072
F32 = jnp.float32
BF16 = jnp.bfloat16
MESH = pl.DeviceIdType.MESH
WINDOW = (-4, -3, -2, -1, 1, 2, 3)
Z_NEAR = (1, 2, 3, 4, 28, 29, 30, 31)


def kernel(
    tok_hbm, gain_hbm, w_hbm, kg_hbm, keys_ref, ig_ref, wg_ref,
    tok_ref, gain_ref, kg_ref, nrm, n2, kg2, inv, ta, tb, ra, rb, sa, sb, ra2, rb2, zbuf, rza, zb2, rzb,
    fsend, frecv, wbuf, sg, acc,
    swap_s, swap_r, gz_s, gz_r, a1_s, a1_r, b1_s, b1_r, a2_s, a2_r, b2_s, b2_r,
    za_s, za_r, zb_s, zb_r, g0p_s, g0p_r, g1p_s, g1p_r, g0q_s, g0q_r, g1q_s, g1q_r,
    fw_s, fw_r, fin_s, fin_r, load_s, far_s,
):
    grp = lax.axis_index("grp")
    inner = lax.axis_index("inner")
    x = grp // 4
    z = (grp % 4) * 8 + (inner // 2) % 8
    y = inner // 16
    c = inner % 2
    oc = 1 - c
    zl = z % 8
    zg = z // 4
    zm = z % 4

    def dev(px, py, pz, pc):
        return (px * 4 + pz // 8, (py * 8 + pz % 8) * 2 + pc)

    sends = []

    def send(src, dst, s, r, target):
        copy = pltpu.make_async_remote_copy(
            src_ref=src, dst_ref=dst, send_sem=s, recv_sem=r,
            device_id=target, device_id_type=MESH,
        )
        copy.start()
        sends.append(copy)
        return copy

    xp = [(x + k) % 4 for k in range(4)]
    yp = [(y + k) % 4 for k in range(4)]
    partner = dev(x, y, z, oc)

    barrier = pltpu.get_barrier_semaphore()
    peers = [partner]
    peers += [dev(xp[k], y, z, c) for k in (1, 2, 3)]
    peers += [dev(x, yp[k], z, c) for k in (1, 2, 3)]
    peers += [dev(x, y, (z + k) % 32, c) for k in Z_NEAR]
    for peer in peers:
        pl.semaphore_signal(barrier, inc=1, device_id=peer, device_id_type=MESH)

    w_own = w_hbm.at[pl.ds(pl.multiple_of(x * 16, 16), 16), :]
    loads = [
        pltpu.make_async_copy(src, dst, load_s.at[n])
        for n, (src, dst) in enumerate(
            (
                (tok_hbm, tok_ref), (gain_hbm, gain_ref), (kg_hbm, kg_ref),
                (w_own, wbuf.at[y, zl, c * 4 + x]),
            )
        )
    ]
    for copy in loads:
        copy.start()
    pl.semaphore_wait(barrier, len(peers))

    gz = []
    for n, k in enumerate(WINDOW):
        gz.append(
            send(
                w_own, wbuf.at[y, zl, c * 4 + x], gz_s.at[n], gz_r.at[n],
                dev(x, y, (z + k) % 32, c),
            )
        )

    for k in (4, 28):
        pl.semaphore_signal(
            far_s.at[0], inc=1, device_id=dev(x, y, (z + k) % 32, c), device_id_type=MESH
        )

    for copy in loads:
        copy.wait()
    kg_copy = send(
        kg_ref.at[:, pl.ds(pl.multiple_of(oc * 256, 256), 256)], kg2.at[c],
        swap_s.at[4], swap_r.at[4], partner,
    )
    kg2[c] = kg_ref[:, pl.ds(pl.multiple_of(c * 256, 256), 256)]
    total = jnp.zeros((TOK, 128), F32)
    for j in range(D // 512):
        v = tok_ref[:, j * 512:(j + 1) * 512].astype(F32)
        v = v * v
        for i in range(4):
            total = total + v[:, i * 128:(i + 1) * 128]
    inverse = lax.rsqrt(jnp.sum(total, axis=-1, keepdims=True) * (1.0 / D) + 1e-05)
    inv[...] = inverse
    order = (2, 1, 3, 0)
    swaps = {}
    for k in order:
        cols = pl.ds(pl.multiple_of(xp[k] * 1024, 1024), 1024)
        v = tok_ref[:, cols].astype(F32) * inverse
        v = (v * gain_ref[:, cols]).astype(BF16)
        nrm[xp[k]] = v
        n2[xp[k], c] = v.T
        piece = n2.at[xp[k], c]
        swaps[k] = send(piece, piece, swap_s.at[k], swap_r.at[k], partner)

    kg_copy.wait_recv()
    a1, b1 = {}, []
    for k in order:
        swaps[k].wait_recv()
        xt = xp[k]
        for j in range(4):
            rows = slice(j * 256, (j + 1) * 256)
            lhs = jnp.concatenate([n2[xt, 0, rows], n2[xt, 1, rows]], axis=1)
            t = jnp.dot(
                lhs, kg2[...].reshape(2 * TOK, 256), preferred_element_type=F32
            ).astype(BF16)
            ta[xt, j] = t[:, :128].reshape(4, 64, 128)
            tb[xt, j] = t[:, 128:].reshape(4, 64, 128)
        if k:
            a1[k] = send(ta.at[xt], ra.at[k - 1], a1_s.at[k - 1], a1_r.at[k - 1], dev(xt, y, z, c))
        for i in (2, 1, 3):
            n = k * 3 + i - 1
            b1.append(
                send(
                    tb.at[xt, :, yp[i]], rb.at[i - 1, (x + k) % 4], b1_s.at[n], b1_r.at[n],
                    dev(x, yp[i], z, c),
                )
            )
    pl.semaphore_wait(far_s.at[0], 2)
    for k in (8, 24):
        pl.semaphore_signal(
            far_s.at[1], inc=1, device_id=dev(x, y, (z + k) % 32, c), device_id_type=MESH
        )

    for copy in gz:
        copy.wait_recv()

    g0p = []
    g1p = []
    for k in (2, 1, 3):
        piece = wbuf.at[y, 0:4, c * 4 + x]
        g0p.append(send(piece, piece, g0p_s.at[k - 1], g0p_r.at[k - 1], dev(xp[k], y, z, c)))
        piece = wbuf.at[y, 4:8, c * 4 + x]
        g1p.append(send(piece, piece, g1p_s.at[k - 1], g1p_r.at[k - 1], dev(x, yp[k], z, c)))

    for k in (1, 3, 2):
        a1[k].wait_recv()
    for j in range(4):
        v = ta[x, j].astype(F32)
        for k in range(3):
            v = v + ra[k, j].astype(F32)
        sa[j] = v.astype(BF16)
    a2 = [
        send(sa.at[:, yp[k]], ra2.at[k - 1], a2_s.at[k - 1], a2_r.at[k - 1], dev(x, yp[k], z, c))
        for k in (2, 1, 3)
    ]
    for copy in b1:
        copy.wait_recv()
    for j in range(4):
        v = tb[j, :, y].astype(F32)
        for k in range(3):
            v = v + rb[k, j].astype(F32)
        sb[j] = v.astype(BF16)
    b2 = [
        send(sb.at[xp[k]], rb2.at[k - 1], b2_s.at[k - 1], b2_r.at[k - 1], dev(xp[k], y, z, c))
        for k in (2, 1, 3)
    ]
    forwards = []

    def forward(piece):
        n = len(forwards)
        forwards.append(send(piece, piece, fw_s.at[n], fw_r.at[n], partner))

    for copy in g0p:
        copy.wait_recv()
    g0q = {}
    for k in (2, 1, 3):
        piece = wbuf.at[y, 0:4, pl.ds(c * 4, 4)]
        g0q[k] = send(piece, piece, g0q_s.at[k - 1], g0q_r.at[k - 1], dev(x, yp[k], z, c))
    for copy in g1p:
        copy.wait_recv()
    g1q = {}
    for k in (2, 1, 3):
        piece = wbuf.at[:, 4:8, c * 4 + x]
        g1q[k] = send(piece, piece, g1q_s.at[k - 1], g1q_r.at[k - 1], dev(xp[k], y, z, c))
    forward(wbuf.at[y, 0:4, pl.ds(c * 4, 4)])
    forward(wbuf.at[:, 4:8, c * 4 + x])

    for copy in a2:
        copy.wait_recv()
    for copy in b2:
        copy.wait_recv()
    fa = sa[:, y].astype(F32)
    fb = sb[x].astype(F32)
    for k in range(3):
        fa = fa + ra2[k].astype(F32)
        fb = fb + rb2[k].astype(F32)
    both = jnp.concatenate([fa.reshape(8, 4, 8, 128), fb.reshape(8, 4, 8, 128)], axis=2)
    zbuf[...] = both.astype(BF16)
    za = [
        send(
            zbuf.at[:, (zm + k) % 4], rza.at[k - 1], za_s.at[k - 1], za_r.at[k - 1],
            dev(x, y, zg * 4 + (zm + k) % 4, c),
        )
        for k in (1, 2, 3)
    ]

    for copy in za:
        copy.wait_recv()
    v = zbuf[:, zm].astype(F32)
    for k in range(3):
        v = v + rza[k].astype(F32)
    zb2[...] = v.astype(BF16)
    pl.semaphore_wait(far_s.at[1], 2)
    zb = []
    for k in (4, 3, 5, 2, 6, 1, 7):
        gt = (zg + k) % 8
        zb.append(
            send(zb2.at[gt], rzb.at[k - 1], zb_s.at[k - 1], zb_r.at[k - 1], dev(x, y, gt * 4 + zm, c))
        )

    for k in (1, 3, 2):
        g0q[k].wait_recv()
        forward(wbuf.at[yp[4 - k], 0:4, pl.ds(c * 4, 4)])
        g1q[k].wait_recv()
        forward(wbuf.at[:, 4:8, c * 4 + xp[4 - k]])

    acc[...] = jnp.zeros_like(acc)
    dots = jnp.zeros((TOK, 128), F32)
    for half in range(2):
        for copy in forwards[half::2]:
            copy.wait_recv()

        def block(j, dots, half=half):
            for i in (2 * half, 2 * half + 1):
                rows = slice(i * 256, (i + 1) * 256)
                w = wbuf[j, i * 2:(i + 1) * 2].reshape(256, KW)
                acc[...] += jnp.dot(nrm[j, :, rows], w, preferred_element_type=F32)
                cols = pl.ds(pl.multiple_of(j * 1024 + i * 256, 256), 256)
                ng = lax.dot_general(
                    kg_ref[...], w, (((1,), (1,)), ((), ())), preferred_element_type=F32
                )
                s = ng * gain_ref[:, cols]
                sg[j, :, rows] = s
                p = s * (tok_ref[:, cols].astype(F32) * inv[...])
                dots = dots + p[:, :128] + p[:, 128:]
            return dots

        dots = lax.fori_loop(0, 4, block, dots)
    keys_ref[...] = acc[...].astype(BF16)
    centre = jnp.sum(dots, axis=-1, keepdims=True) * (1.0 / D)

    def finish(j, carry):
        cols = pl.ds(pl.multiple_of(j * 1024, 1024), 1024)
        unit = tok_ref[:, cols].astype(F32) * inv[...]
        ig_ref[:, cols] = ((sg[j] - unit * centre) * inv[...]).astype(BF16)
        return carry

    lax.fori_loop(0, 4, finish, 0)

    for copy in zb:
        copy.wait_recv()
    v = zb2[zg].astype(F32)
    for k in range(7):
        v = v + rzb[k].astype(F32)
    v = v * (TOKENS ** -0.5)
    low = jnp.concatenate([v[0:4], v[8:12]], axis=0)
    high = jnp.concatenate([v[4:8], v[12:16]], axis=0)
    mine = jnp.where(c == 0, low, high)
    fsend[...] = jnp.where(c == 0, high, low)
    fin = send(fsend, frecv, fin_s.at[0], fin_r.at[0], partner)

    fin.wait_recv()
    other = frecv[...]
    first = jnp.where(c == 0, mine, other)
    second = jnp.where(c == 0, other, mine)
    wg_ref[:, 0:128] = first[0:4]
    wg_ref[:, 128:256] = first[4:8]
    wg_ref[:, 256:384] = second[0:4]
    wg_ref[:, 384:512] = second[4:8]

    for copy in sends:
        copy.wait_send()


def place(keys_in, ig_in, wg_in, keys_out, ig_out, wg_out, keys_buf, ig_buf, wg_buf, sem):
    parts = [(ig_in, ig_buf, ig_out, pl.ds(n * 32, 32)) for n in range(4)]
    parts += [(keys_in, keys_buf, keys_out, pl.ds(0, TOK)), (wg_in, wg_buf, wg_out, pl.ds(0, 4))]
    reads = []
    writes = []
    for n, (src, buf, dst, rows) in enumerate(parts):
        reads.append(pltpu.make_async_copy(src.at[rows], buf.at[rows], sem.at[n]))
        writes.append(pltpu.make_async_copy(buf.at[rows], dst.at[rows], sem.at[6 + n]))
    for copy in reads:
        copy.start()
    for n in range(6):
        reads[n].wait()
        writes[n].start()
    for copy in writes:
        copy.wait()


def shards(tokens, norm_gain, key_weight, key_grad):
    vmem = pl.BlockSpec(memory_space=pltpu.VMEM)
    hbm = pl.BlockSpec(memory_space=pl.ANY)
    pairs = (5, 7, 3, 12, 3, 3, 3, 7, 3, 3, 3, 3, 8, 1)
    sems = []
    for n in pairs:
        sems += [pltpu.SemaphoreType.DMA((n,)), pltpu.SemaphoreType.DMA((n,))]
    shapes = (
        jax.ShapeDtypeStruct((TOK, KW), BF16),
        jax.ShapeDtypeStruct((TOK, D), BF16),
        jax.ShapeDtypeStruct((4, KW), F32),
    )
    results = pl.pallas_call(
        kernel,
        name="key_projection",
        out_shape=shapes,
        in_specs=[hbm] * 4,
        out_specs=(vmem, vmem, vmem),
        scratch_shapes=[
            pltpu.VMEM((TOK, D), BF16),
            pltpu.VMEM((1, D), F32),
            pltpu.VMEM((TOK, KW), BF16),
            pltpu.VMEM((4, TOK, 1024), BF16),
            pltpu.VMEM((4, 2, 1024, TOK), BF16),
            pltpu.VMEM((2, TOK, 256), BF16),
            pltpu.VMEM((TOK, 1), F32),
            pltpu.VMEM((4, 4, 4, 64, 128), BF16),
            pltpu.VMEM((4, 4, 4, 64, 128), BF16),
            pltpu.VMEM((3, 4, 4, 64, 128), BF16),
            pltpu.VMEM((3, 4, 4, 64, 128), BF16),
            pltpu.VMEM((4, 4, 64, 128), BF16),
            pltpu.VMEM((4, 4, 64, 128), BF16),
            pltpu.VMEM((3, 4, 64, 128), BF16),
            pltpu.VMEM((3, 4, 64, 128), BF16),
            pltpu.VMEM((8, 4, 16, 128), BF16),
            pltpu.VMEM((3, 8, 16, 128), BF16),
            pltpu.VMEM((8, 16, 128), BF16),
            pltpu.VMEM((7, 16, 128), BF16),
            pltpu.VMEM((8, 128), F32),
            pltpu.VMEM((8, 128), F32),
            pltpu.VMEM((4, 8, 8, 16, KW), BF16),
            pltpu.VMEM((4, TOK, 1024), F32),
            pltpu.VMEM((TOK, KW), F32),
        ] + sems + [pltpu.SemaphoreType.DMA((4,)), pltpu.SemaphoreType.REGULAR((2,))],
        compiler_params=pltpu.CompilerParams(
            collective_id=0, has_side_effects=True, vmem_limit_bytes=60 * 2**20
        ),
    )(tokens, norm_gain.reshape(1, D), key_weight, key_grad)
    return pl.pallas_call(
        place,
        name="place_results",
        out_shape=shapes,
        in_specs=[hbm] * 3,
        out_specs=(hbm, hbm, hbm),
        scratch_shapes=[
            pltpu.VMEM((TOK, KW), BF16),
            pltpu.VMEM((TOK, D), BF16),
            pltpu.VMEM((4, KW), F32),
            pltpu.SemaphoreType.DMA((12,)),
        ],
        compiler_params=pltpu.CompilerParams(vmem_limit_bytes=60 * 2**20),
    )(*results)


def solution(mesh):
    return jax.shard_map(
        shards,
        mesh=mesh,
        in_specs=(P(("grp", "inner"), None), P(), P("inner", None), P(("grp", "inner"), None)),
        out_specs=(P(("grp", "inner"), None), P(("grp", "inner"), None), P(("grp", "inner"), None)),
        check_vma=False,
    )
```

time: 83.6 us -> 71.3 us (0.85)
  the two profiles are of different devices: /device:TPU:1 before, /device:TPU:9 now
where the time goes in v2:
time: 71.3 us; the launch traced here: 71.2 us
  Pallas kernels  70.5 us (99%)
    pallas_call x1, Pallas kernels, shards(): pl.pallas_call(kernel, name='key_projection', out_shape=shapes, in_specs=...  68.5 us
    pallas_call x1, Pallas kernels, shards(): pl.pallas_call(place, name='place_results', out_shape=shapes, in_specs=[h...  2.06 us

profile of v2, /device:TPU:9, one launch (start us, length us, event | category | flops | bytes accessed | tf_op | source)
XLA Modules:
  0.0 71.2 jit_solution(11733710642447588032)
XLA Ops:
  0.6 68.5 %key_projection.1 = (bf16[128,512]{1,0:T(8,128)(2,1)}, bf16[128,4096]{1,0:T(8,128)(2,1)}, f32[4,512]{1,0:T(4,128)}) custom-call(bf16[128,4096]{1,0:T(8,128)(2,1)} %tok_hbm.1, f32[1,4096]{1,0:T(1,128)} %bitcast.1, bf16[64,512]{1,0:T(8,128)(2,1)} %w_hbm.1, bf16[128,512]{1,0:T(8,128)(2,1)} %kg_hbm.1), custom_call_target="tpu_custom_call" | custom-call | tf_op jit(solution)/shard_map/key_projection/pallas_call | solution.py:329
  69.1 2.1 %place_results.1 = (bf16[128,512]{1,0:T(8,128)(2,1)}, bf16[128,4096]{1,0:T(8,128)(2,1)}, f32[4,512]{1,0:T(4,128)}) custom-call(bf16[128,512]{1,0:T(8,128)(2,1)} %get-tuple-element.6.keys_in, bf16[128,4096]{1,0:T(8,128)(2,1)} %get-tuple-element.7.ig_in, f32[4,512]{1,0:T(4,128)} %get-tuple-element.8.wg_in), custom_call_target="tpu_custom_call" | custom-call | tf_op jit(solution)/shard_map/place_results/pallas_call | solution.py:365

commit v3 on v2

--- a/solution.py
+++ b/solution.py
@@ -19,12 +19,13 @@
 
 
 def kernel(
-    tok_hbm, gain_hbm, w_hbm, kg_hbm, keys_ref, ig_ref, wg_ref,
+    tok_hbm, gain_hbm, w_hbm, kg_hbm, keys_hbm, ig_hbm, wg_ref,
+    keys_ref, ig_ref,
     tok_ref, gain_ref, kg_ref, nrm, n2, kg2, inv, ta, tb, ra, rb, sa, sb, ra2, rb2, zbuf, rza, zb2, rzb,
     fsend, frecv, wbuf, sg, acc,
     swap_s, swap_r, gz_s, gz_r, a1_s, a1_r, b1_s, b1_r, a2_s, a2_r, b2_s, b2_r,
     za_s, za_r, zb_s, zb_r, g0p_s, g0p_r, g1p_s, g1p_r, g0q_s, g0q_r, g1q_s, g1q_r,
-    fw_s, fw_r, fin_s, fin_r, load_s, far_s,
+    fw_s, fw_r, fin_s, fin_r, load_s, far_s, out_s,
 ):
     grp = lax.axis_index("grp")
     inner = lax.axis_index("inner")
@@ -75,28 +76,8 @@
     ]
     for copy in loads:
         copy.start()
-    pl.semaphore_wait(barrier, len(peers))
-
-    gz = []
-    for n, k in enumerate(WINDOW):
-        gz.append(
-            send(
-                w_own, wbuf.at[y, zl, c * 4 + x], gz_s.at[n], gz_r.at[n],
-                dev(x, y, (z + k) % 32, c),
-            )
-        )
-
-    for k in (4, 28):
-        pl.semaphore_signal(
-            far_s.at[0], inc=1, device_id=dev(x, y, (z + k) % 32, c), device_id_type=MESH
-        )
-
     for copy in loads:
         copy.wait()
-    kg_copy = send(
-        kg_ref.at[:, pl.ds(pl.multiple_of(oc * 256, 256), 256)], kg2.at[c],
-        swap_s.at[4], swap_r.at[4], partner,
-    )
     kg2[c] = kg_ref[:, pl.ds(pl.multiple_of(c * 256, 256), 256)]
     total = jnp.zeros((TOK, 128), F32)
     for j in range(D // 512):
@@ -108,14 +89,43 @@
     inv[...] = inverse
     order = (2, 1, 3, 0)
     swaps = {}
-    for k in order:
+
+    def norm_block(k):
         cols = pl.ds(pl.multiple_of(xp[k] * 1024, 1024), 1024)
         v = tok_ref[:, cols].astype(F32) * inverse
         v = (v * gain_ref[:, cols]).astype(BF16)
         nrm[xp[k]] = v
         n2[xp[k], c] = v.T
+
+    def swap_block(k):
         piece = n2.at[xp[k], c]
         swaps[k] = send(piece, piece, swap_s.at[k], swap_r.at[k], partner)
+
+    norm_block(order[0])
+    pl.semaphore_wait(barrier, len(peers))
+    kg_copy = send(
+        kg_ref.at[:, pl.ds(pl.multiple_of(oc * 256, 256), 256)], kg2.at[c],
+        swap_s.at[4], swap_r.at[4], partner,
+    )
+    swap_block(order[0])
+
+    gz = []
+    for n, k in enumerate(WINDOW):
+        gz.append(
+            send(
+                w_own, wbuf.at[y, zl, c * 4 + x], gz_s.at[n], gz_r.at[n],
+                dev(x, y, (z + k) % 32, c),
+            )
+        )
+
+    for k in (4, 28):
+        pl.semaphore_signal(
+            far_s.at[0], inc=1, device_id=dev(x, y, (z + k) % 32, c), device_id_type=MESH
+        )
+
+    for k in order[1:]:
+        norm_block(k)
+        swap_block(k)
 
     kg_copy.wait_recv()
     a1, b1 = {}, []
@@ -185,16 +195,12 @@
         n = len(forwards)
         forwards.append(send(piece, piece, fw_s.at[n], fw_r.at[n], partner))
 
-    for copy in g0p:
-        copy.wait_recv()
-    g0q = {}
-    for k in (2, 1, 3):
+    for copy in g0p + g1p:
+        copy.wait_recv()
+    g0q, g1q = {}, {}
+    for k in (1,):
         piece = wbuf.at[y, 0:4, pl.ds(c * 4, 4)]
         g0q[k] = send(piece, piece, g0q_s.at[k - 1], g0q_r.at[k - 1], dev(x, yp[k], z, c))
-    for copy in g1p:
-        copy.wait_recv()
-    g1q = {}
-    for k in (2, 1, 3):
         piece = wbuf.at[:, 4:8, c * 4 + x]
         g1q[k] = send(piece, piece, g1q_s.at[k - 1], g1q_r.at[k - 1], dev(xp[k], y, z, c))
     forward(wbuf.at[y, 0:4, pl.ds(c * 4, 4)])
@@ -218,6 +224,12 @@
         )
         for k in (1, 2, 3)
     ]
+
+    for k in (3, 2):
+        piece = wbuf.at[y, 0:4, pl.ds(c * 4, 4)]
+        g0q[k] = send(piece, piece, g0q_s.at[k - 1], g0q_r.at[k - 1], dev(x, yp[k], z, c))
+        piece = wbuf.at[:, 4:8, c * 4 + x]
+        g1q[k] = send(piece, piece, g1q_s.at[k - 1], g1q_r.at[k - 1], dev(xp[k], y, z, c))
 
     for copy in za:
         copy.wait_recv()
@@ -271,6 +283,12 @@
         return carry
 
     lax.fori_loop(0, 4, finish, 0)
+    results = [
+        pltpu.make_async_copy(keys_ref, keys_hbm, out_s.at[0]),
+        pltpu.make_async_copy(ig_ref, ig_hbm, out_s.at[1]),
+    ]
+    for copy in results:
+        copy.start()
 
     for copy in zb:
         copy.wait_recv()
@@ -295,6 +313,8 @@
 
     for copy in sends:
         copy.wait_send()
+    for copy in results:
+        copy.wait()
 
 
 def place(keys_in, ig_in, wg_in, keys_out, ig_out, wg_out, keys_buf, ig_buf, wg_buf, sem):
@@ -331,8 +351,10 @@
         name="key_projection",
         out_shape=shapes,
         in_specs=[hbm] * 4,
-        out_specs=(vmem, vmem, vmem),
+        out_specs=(hbm, hbm, vmem),
         scratch_shapes=[
+            pltpu.VMEM((TOK, KW), BF16),
+            pltpu.VMEM((TOK, D), BF16),
             pltpu.VMEM((TOK, D), BF16),
             pltpu.VMEM((1, D), F32),
             pltpu.VMEM((TOK, KW), BF16),
@@ -357,7 +379,8 @@
             pltpu.VMEM((4, 8, 8, 16, KW), BF16),
             pltpu.VMEM((4, TOK, 1024), F32),
             pltpu.VMEM((TOK, KW), F32),
-        ] + sems + [pltpu.SemaphoreType.DMA((4,)), pltpu.SemaphoreType.REGULAR((2,))],
+        ] + sems + [pltpu.SemaphoreType.DMA((4,)), pltpu.SemaphoreType.REGULAR((2,))]
+        + [pltpu.SemaphoreType.DMA((2,))],
         compiler_params=pltpu.CompilerParams(
             collective_id=0, has_side_effects=True, vmem_limit_bytes=60 * 2**20
         ),

time: 71.3 us -> 67.8 us (0.951)
  the two profiles are of different devices: /device:TPU:9 before, /device:TPU:1 now
where the time goes in v3:
time: 67.8 us; the launch traced here: 67.6 us
  Pallas kernels  67 us (99%)
    pallas_call x1, Pallas kernels, shards(): pl.pallas_call(kernel, name='key_projection', out_shape=shapes, in_specs=...  64.9 us
    pallas_call x1, Pallas kernels, shards(): pl.pallas_call(place, name='place_results', out_shape=shapes, in_specs=[h...  2.06 us

profile of v3, /device:TPU:1, one launch (start us, length us, event | category | flops | bytes accessed | tf_op | source)
XLA Modules:
  0.0 67.6 jit_solution(2837172628695343740)
XLA Ops:
  0.6 64.9 %key_projection.1 = (bf16[128,512]{1,0:T(8,128)(2,1)}, bf16[128,4096]{1,0:T(8,128)(2,1)}, f32[4,512]{1,0:T(4,128)}) custom-call(bf16[128,4096]{1,0:T(8,128)(2,1)} %tok_hbm.1, f32[1,4096]{1,0:T(1,128)} %bitcast.1, bf16[64,512]{1,0:T(8,128)(2,1)} %w_hbm.1, bf16[128,512]{1,0:T(8,128)(2,1)} %kg_hbm.1), custom_call_target="tpu_custom_call" | custom-call | tf_op jit(solution)/shard_map/key_projection/pallas_call | solution.py:349
  65.5 2.1 %place_results.1 = (bf16[128,512]{1,0:T(8,128)(2,1)}, bf16[128,4096]{1,0:T(8,128)(2,1)}, f32[4,512]{1,0:T(4,128)}) custom-call(bf16[128,512]{1,0:T(8,128)(2,1)} %get-tuple-element.6.keys_in, bf16[128,4096]{1,0:T(8,128)(2,1)} %get-tuple-element.7.ig_in, f32[4,512]{1,0:T(4,128)} %get-tuple-element.8.wg_in), custom_call_target="tpu_custom_call" | custom-call | tf_op jit(solution)/shard_map/place_results/pallas_call | solution.py:388

commit v4 on v3

--- a/solution.py
+++ b/solution.py
@@ -21,11 +21,11 @@
 def kernel(
     tok_hbm, gain_hbm, w_hbm, kg_hbm, keys_hbm, ig_hbm, wg_ref,
     keys_ref, ig_ref,
-    tok_ref, gain_ref, kg_ref, nrm, n2, kg2, inv, ta, tb, ra, rb, sa, sb, ra2, rb2, zbuf, rza, zb2, rzb,
-    fsend, frecv, wbuf, sg, acc,
+    tok_ref, gain_ref, kg_ref, nrm, n2, n2_out, kg2, inv, ta, tb, ra, rb, sa, sb, ra2, rb2, zbuf, rza, zb2, rzb,
+    wbuf, sg, acc,
     swap_s, swap_r, gz_s, gz_r, a1_s, a1_r, b1_s, b1_r, a2_s, a2_r, b2_s, b2_r,
     za_s, za_r, zb_s, zb_r, g0p_s, g0p_r, g1p_s, g1p_r, g0q_s, g0q_r, g1q_s, g1q_r,
-    fw_s, fw_r, fin_s, fin_r, load_s, far_s, out_s,
+    fw_s, fw_r, load_s, far_s, out_s,
 ):
     grp = lax.axis_index("grp")
     inner = lax.axis_index("inner")
@@ -69,43 +69,58 @@
         pltpu.make_async_copy(src, dst, load_s.at[n])
         for n, (src, dst) in enumerate(
             (
-                (tok_hbm, tok_ref), (gain_hbm, gain_ref), (kg_hbm, kg_ref),
-                (w_own, wbuf.at[y, zl, c * 4 + x]),
+                *(
+                    (tok_hbm.at[:, pl.ds(j * 1024, 1024)], tok_ref.at[:, pl.ds(j * 1024, 1024)])
+                    for j in range(4)
+                ),
+                (kg_hbm, kg_ref), (gain_hbm, gain_ref), (w_own, wbuf.at[y, zl, c * 4 + x]),
             )
         )
     ]
     for copy in loads:
         copy.start()
-    for copy in loads:
+    total = jnp.zeros((TOK, 128), F32)
+    for j in range(4):
+        loads[j].wait()
+        for i in range(8):
+            v = tok_ref[:, j * 1024 + i * 128:j * 1024 + (i + 1) * 128].astype(F32)
+            total = total + v * v
+    for copy in loads[4:]:
         copy.wait()
-    kg2[c] = kg_ref[:, pl.ds(pl.multiple_of(c * 256, 256), 256)]
-    total = jnp.zeros((TOK, 128), F32)
-    for j in range(D // 512):
-        v = tok_ref[:, j * 512:(j + 1) * 512].astype(F32)
-        v = v * v
-        for i in range(4):
-            total = total + v[:, i * 128:(i + 1) * 128]
+    kg2[c] = kg_ref[...]
     inverse = lax.rsqrt(jnp.sum(total, axis=-1, keepdims=True) * (1.0 / D) + 1e-05)
     inv[...] = inverse
     order = (2, 1, 3, 0)
     swaps = {}
+
+    row = lax.broadcasted_iota(jnp.int32, (128, 256), 0)
+    feature = lax.broadcasted_iota(jnp.int32, (128, 256), 1)
+    first = (row // 4) * 8 + row % 4
+    own_rows = jnp.where(feature == first + c * 4, 1.0, 0.0).astype(BF16)
+    other_rows = jnp.where(feature == first + oc * 4, 1.0, 0.0).astype(BF16)
+
+    def picked(rows, v):
+        return lax.dot_general(
+            rows, v, (((1,), (1,)), ((), ())), preferred_element_type=F32
+        ).astype(BF16)
 
     def norm_block(k):
         cols = pl.ds(pl.multiple_of(xp[k] * 1024, 1024), 1024)
         v = tok_ref[:, cols].astype(F32) * inverse
         v = (v * gain_ref[:, cols]).astype(BF16)
         nrm[xp[k]] = v
-        n2[xp[k], c] = v.T
+        for j in range(4):
+            part = v[:, j * 256:(j + 1) * 256]
+            n2_out[xp[k], j * 128:(j + 1) * 128] = picked(other_rows, part)
+            n2[xp[k], c, j * 128:(j + 1) * 128] = picked(own_rows, part)
 
     def swap_block(k):
-        piece = n2.at[xp[k], c]
-        swaps[k] = send(piece, piece, swap_s.at[k], swap_r.at[k], partner)
+        swaps[k] = send(n2_out.at[xp[k]], n2.at[xp[k], c], swap_s.at[k], swap_r.at[k], partner)
 
     norm_block(order[0])
     pl.semaphore_wait(barrier, len(peers))
     kg_copy = send(
-        kg_ref.at[:, pl.ds(pl.multiple_of(oc * 256, 256), 256)], kg2.at[c],
-        swap_s.at[4], swap_r.at[4], partner,
+        kg_ref, kg2.at[c], swap_s.at[4], swap_r.at[4], partner,
     )
     swap_block(order[0])
 
@@ -123,23 +138,22 @@
             far_s.at[0], inc=1, device_id=dev(x, y, (z + k) % 32, c), device_id_type=MESH
         )
 
-    for k in order[1:]:
-        norm_block(k)
-        swap_block(k)
+    norm_block(order[1])
+    swap_block(order[1])
 
     kg_copy.wait_recv()
     a1, b1 = {}, []
-    for k in order:
+    for step, k in enumerate(order):
         swaps[k].wait_recv()
         xt = xp[k]
         for j in range(4):
-            rows = slice(j * 256, (j + 1) * 256)
+            rows = slice(j * 128, (j + 1) * 128)
             lhs = jnp.concatenate([n2[xt, 0, rows], n2[xt, 1, rows]], axis=1)
             t = jnp.dot(
-                lhs, kg2[...].reshape(2 * TOK, 256), preferred_element_type=F32
+                lhs, kg2[...].reshape(2 * TOK, KW), preferred_element_type=F32
             ).astype(BF16)
-            ta[xt, j] = t[:, :128].reshape(4, 64, 128)
-            tb[xt, j] = t[:, 128:].reshape(4, 64, 128)
+            ta[xt, j] = t[:, :256].reshape(4, 32, 256)
+            tb[xt, j] = t[:, 256:].reshape(4, 32, 256)
         if k:
             a1[k] = send(ta.at[xt], ra.at[k - 1], a1_s.at[k - 1], a1_r.at[k - 1], dev(xt, y, z, c))
         for i in (2, 1, 3):
@@ -150,6 +164,9 @@
                     dev(x, yp[i], z, c),
                 )
             )
+        if step + 2 < 4:
+            norm_block(order[step + 2])
+            swap_block(order[step + 2])
     pl.semaphore_wait(far_s.at[0], 2)
     for k in (8, 24):
         pl.semaphore_signal(
@@ -215,8 +232,17 @@
     for k in range(3):
         fa = fa + ra2[k].astype(F32)
         fb = fb + rb2[k].astype(F32)
-    both = jnp.concatenate([fa.reshape(8, 4, 8, 128), fb.reshape(8, 4, 8, 128)], axis=2)
-    zbuf[...] = both.astype(BF16)
+    for zh in range(4):
+        for n in range(8):
+            four = slice(n * 4, (n + 1) * 4)
+            chunk = jnp.concatenate(
+                [
+                    fa[zh, four, :128], fa[zh, four, 128:],
+                    fb[zh, four, :128], fb[zh, four, 128:],
+                ],
+                axis=0,
+            )
+            zbuf[zh * 2 + n // 4, n % 4] = chunk.astype(BF16)
     za = [
         send(
             zbuf.at[:, (zm + k) % 4], rza.at[k - 1], za_s.at[k - 1], za_r.at[k - 1],
@@ -245,34 +271,41 @@
             send(zb2.at[gt], rzb.at[k - 1], zb_s.at[k - 1], zb_r.at[k - 1], dev(x, y, gt * 4 + zm, c))
         )
 
+    acc[...] = jnp.zeros_like(acc)
+
+    def block(j, half, dots):
+        for i in (2 * half, 2 * half + 1):
+            rows = slice(i * 256, (i + 1) * 256)
+            w = wbuf[j, i * 2:(i + 1) * 2].reshape(256, KW)
+            acc[...] += jnp.dot(nrm[j, :, rows], w, preferred_element_type=F32)
+            cols = pl.ds(pl.multiple_of(j * 1024 + i * 256, 256), 256)
+            ng = lax.dot_general(
+                kg_ref[...], w, (((1,), (1,)), ((), ())), preferred_element_type=F32
+            )
+            s = ng * gain_ref[:, cols]
+            sg[j, :, rows] = s
+            p = s * (tok_ref[:, cols].astype(F32) * inv[...])
+            dots = dots + p[:, :128] + p[:, 128:]
+        return dots
+
+    dots = jnp.zeros((TOK, 128), F32)
     for k in (1, 3, 2):
         g0q[k].wait_recv()
         forward(wbuf.at[yp[4 - k], 0:4, pl.ds(c * 4, 4)])
         g1q[k].wait_recv()
         forward(wbuf.at[:, 4:8, c * 4 + xp[4 - k]])
-
-    acc[...] = jnp.zeros_like(acc)
-    dots = jnp.zeros((TOK, 128), F32)
-    for half in range(2):
-        for copy in forwards[half::2]:
-            copy.wait_recv()
-
-        def block(j, dots, half=half):
-            for i in (2 * half, 2 * half + 1):
-                rows = slice(i * 256, (i + 1) * 256)
-                w = wbuf[j, i * 2:(i + 1) * 2].reshape(256, KW)
-                acc[...] += jnp.dot(nrm[j, :, rows], w, preferred_element_type=F32)
-                cols = pl.ds(pl.multiple_of(j * 1024 + i * 256, 256), 256)
-                ng = lax.dot_general(
-                    kg_ref[...], w, (((1,), (1,)), ((), ())), preferred_element_type=F32
-                )
-                s = ng * gain_ref[:, cols]
-                sg[j, :, rows] = s
-                p = s * (tok_ref[:, cols].astype(F32) * inv[...])
-                dots = dots + p[:, :128] + p[:, 128:]
-            return dots
-
-        dots = lax.fori_loop(0, 4, block, dots)
+        if k == 1:
+            forwards[0].wait_recv()
+            dots = block(y, 0, dots)
+        if k == 3:
+            forwards[2].wait_recv()
+            dots = block(yp[3], 0, dots)
+    for n, k in ((4, 3), (6, 2)):
+        forwards[n].wait_recv()
+        dots = block(yp[4 - k], 0, dots)
+    for copy in forwards[1::2]:
+        copy.wait_recv()
+    dots = lax.fori_loop(0, 4, lambda j, d: block(j, 1, d), dots)
     keys_ref[...] = acc[...].astype(BF16)
     centre = jnp.sum(dots, axis=-1, keepdims=True) * (1.0 / D)
 
@@ -296,20 +329,8 @@
     for k in range(7):
         v = v + rzb[k].astype(F32)
     v = v * (TOKENS ** -0.5)
-    low = jnp.concatenate([v[0:4], v[8:12]], axis=0)
-    high = jnp.concatenate([v[4:8], v[12:16]], axis=0)
-    mine = jnp.where(c == 0, low, high)
-    fsend[...] = jnp.where(c == 0, high, low)
-    fin = send(fsend, frecv, fin_s.at[0], fin_r.at[0], partner)
-
-    fin.wait_recv()
-    other = frecv[...]
-    first = jnp.where(c == 0, mine, other)
-    second = jnp.where(c == 0, other, mine)
-    wg_ref[:, 0:128] = first[0:4]
-    wg_ref[:, 128:256] = first[4:8]
-    wg_ref[:, 256:384] = second[0:4]
-    wg_ref[:, 384:512] = second[4:8]
+    for n in range(4):
+        wg_ref[:, n * 128:(n + 1) * 128] = v[n * 4:(n + 1) * 4]
 
     for copy in sends:
         copy.wait_send()
@@ -337,7 +358,7 @@
 def shards(tokens, norm_gain, key_weight, key_grad):
     vmem = pl.BlockSpec(memory_space=pltpu.VMEM)
     hbm = pl.BlockSpec(memory_space=pl.ANY)
-    pairs = (5, 7, 3, 12, 3, 3, 3, 7, 3, 3, 3, 3, 8, 1)
+    pairs = (5, 7, 3, 12, 3, 3, 3, 7, 3, 3, 3, 3, 8)
     sems = []
     for n in pairs:
         sems += [pltpu.SemaphoreType.DMA((n,)), pltpu.SemaphoreType.DMA((n,))]
@@ -359,27 +380,26 @@
             pltpu.VMEM((1, D), F32),
             pltpu.VMEM((TOK, KW), BF16),
             pltpu.VMEM((4, TOK, 1024), BF16),
-            pltpu.VMEM((4, 2, 1024, TOK), BF16),
-            pltpu.VMEM((2, TOK, 256), BF16),
+            pltpu.VMEM((4, 2, 512, TOK), BF16),
+            pltpu.VMEM((4, 512, TOK), BF16),
+            pltpu.VMEM((2, TOK, KW), BF16),
             pltpu.VMEM((TOK, 1), F32),
-            pltpu.VMEM((4, 4, 4, 64, 128), BF16),
-            pltpu.VMEM((4, 4, 4, 64, 128), BF16),
-            pltpu.VMEM((3, 4, 4, 64, 128), BF16),
-            pltpu.VMEM((3, 4, 4, 64, 128), BF16),
-            pltpu.VMEM((4, 4, 64, 128), BF16),
-            pltpu.VMEM((4, 4, 64, 128), BF16),
-            pltpu.VMEM((3, 4, 64, 128), BF16),
-            pltpu.VMEM((3, 4, 64, 128), BF16),
+            pltpu.VMEM((4, 4, 4, 32, 256), BF16),
+            pltpu.VMEM((4, 4, 4, 32, 256), BF16),
+            pltpu.VMEM((3, 4, 4, 32, 256), BF16),
+            pltpu.VMEM((3, 4, 4, 32, 256), BF16),
+            pltpu.VMEM((4, 4, 32, 256), BF16),
+            pltpu.VMEM((4, 4, 32, 256), BF16),
+            pltpu.VMEM((3, 4, 32, 256), BF16),
+            pltpu.VMEM((3, 4, 32, 256), BF16),
             pltpu.VMEM((8, 4, 16, 128), BF16),
             pltpu.VMEM((3, 8, 16, 128), BF16),
             pltpu.VMEM((8, 16, 128), BF16),
             pltpu.VMEM((7, 16, 128), BF16),
-            pltpu.VMEM((8, 128), F32),
-            pltpu.VMEM((8, 128), F32),
             pltpu.VMEM((4, 8, 8, 16, KW), BF16),
             pltpu.VMEM((4, TOK, 1024), F32),
             pltpu.VMEM((TOK, KW), F32),
-        ] + sems + [pltpu.SemaphoreType.DMA((4,)), pltpu.SemaphoreType.REGULAR((2,))]
+        ] + sems + [pltpu.SemaphoreType.DMA((7,)), pltpu.SemaphoreType.REGULAR((2,))]
         + [pltpu.SemaphoreType.DMA((2,))],
         compiler_params=pltpu.CompilerParams(
             collective_id=0, has_side_effects=True, vmem_limit_bytes=60 * 2**20

time: 67.8 us -> 66.2 us (0.976); the launches traced: 67.6 us -> 65.2 us
  Pallas kernels: 67 us -> 64.5 us
    pallas_call x1, Pallas kernels: 64.9 us -> 62.5 us  [shards(): pl.pallas_call(kernel, name='key_projection', out_shape=shapes, in_specs=...]
where the time goes in v4:
time: 66.2 us; the launch traced here: 65.2 us
  Pallas kernels  64.5 us (97%)
    pallas_call x1, Pallas kernels, shards(): pl.pallas_call(kernel, name='key_projection', out_shape=shapes, in_specs=...  62.5 us
    pallas_call x1, Pallas kernels, shards(): pl.pallas_call(place, name='place_results', out_shape=shapes, in_specs=[h...  2.06 us

profile of v4, /device:TPU:1, one launch (start us, length us, event | category | flops | bytes accessed | tf_op | source)
XLA Modules:
  0.0 65.2 jit_solution(3499954980603515521)
XLA Ops:
  0.6 62.5 %key_projection.1 = (bf16[128,512]{1,0:T(8,128)(2,1)}, bf16[128,4096]{1,0:T(8,128)(2,1)}, f32[4,512]{1,0:T(4,128)}) custom-call(bf16[128,4096]{1,0:T(8,128)(2,1)} %tok_hbm.1, f32[1,4096]{1,0:T(1,128)} %bitcast.1, bf16[64,512]{1,0:T(8,128)(2,1)} %w_hbm.1, bf16[128,512]{1,0:T(8,128)(2,1)} %kg_hbm.1), custom_call_target="tpu_custom_call" | custom-call | tf_op jit(solution)/shard_map/key_projection/pallas_call | solution.py:370
  63.1 2.1 %place_results.1 = (bf16[128,512]{1,0:T(8,128)(2,1)}, bf16[128,4096]{1,0:T(8,128)(2,1)}, f32[4,512]{1,0:T(4,128)}) custom-call(bf16[128,512]{1,0:T(8,128)(2,1)} %get-tuple-element.6.keys_in, bf16[128,4096]{1,0:T(8,128)(2,1)} %get-tuple-element.7.ig_in, f32[4,512]{1,0:T(4,128)} %get-tuple-element.8.wg_in), custom_call_target="tpu_custom_call" | custom-call | tf_op jit(solution)/shard_map/place_results/pallas_call | solution.py:408

commit v5 on v4

--- a/solution.py
+++ b/solution.py
@@ -15,7 +15,7 @@
 BF16 = jnp.bfloat16
 MESH = pl.DeviceIdType.MESH
 WINDOW = (-4, -3, -2, -1, 1, 2, 3)
-Z_NEAR = (1, 2, 3, 4, 28, 29, 30, 31)
+Z_NEAR = (1, 2, 30, 31)
 
 
 def kernel(
@@ -124,16 +124,7 @@
     )
     swap_block(order[0])
 
-    gz = []
-    for n, k in enumerate(WINDOW):
-        gz.append(
-            send(
-                w_own, wbuf.at[y, zl, c * 4 + x], gz_s.at[n], gz_r.at[n],
-                dev(x, y, (z + k) % 32, c),
-            )
-        )
-
-    for k in (4, 28):
+    for k in (2, 30):
         pl.semaphore_signal(
             far_s.at[0], inc=1, device_id=dev(x, y, (z + k) % 32, c), device_id_type=MESH
         )
@@ -164,13 +155,28 @@
                     dev(x, yp[i], z, c),
                 )
             )
+        if step == 0:
+            pl.semaphore_wait(far_s.at[0], 2)
+            for k4 in (4, 28):
+                pl.semaphore_signal(
+                    far_s.at[1], inc=1, device_id=dev(x, y, (z + k4) % 32, c), device_id_type=MESH
+                )
+
+            gz = []
+            for n, far in enumerate(WINDOW):
+                gz.append(
+                    send(
+                        w_own, wbuf.at[y, zl, c * 4 + x], gz_s.at[n], gz_r.at[n],
+                        dev(x, y, (z + far) % 32, c),
+                    )
+                )
         if step + 2 < 4:
             norm_block(order[step + 2])
             swap_block(order[step + 2])
-    pl.semaphore_wait(far_s.at[0], 2)
+    pl.semaphore_wait(far_s.at[1], 2)
     for k in (8, 24):
         pl.semaphore_signal(
-            far_s.at[1], inc=1, device_id=dev(x, y, (z + k) % 32, c), device_id_type=MESH
+            far_s.at[2], inc=1, device_id=dev(x, y, (z + k) % 32, c), device_id_type=MESH
         )
 
     for copy in gz:
@@ -263,7 +269,7 @@
     for k in range(3):
         v = v + rza[k].astype(F32)
     zb2[...] = v.astype(BF16)
-    pl.semaphore_wait(far_s.at[1], 2)
+    pl.semaphore_wait(far_s.at[2], 2)
     zb = []
     for k in (4, 3, 5, 2, 6, 1, 7):
         gt = (zg + k) % 8
@@ -399,7 +405,7 @@
             pltpu.VMEM((4, 8, 8, 16, KW), BF16),
             pltpu.VMEM((4, TOK, 1024), F32),
             pltpu.VMEM((TOK, KW), F32),
-        ] + sems + [pltpu.SemaphoreType.DMA((7,)), pltpu.SemaphoreType.REGULAR((2,))]
+        ] + sems + [pltpu.SemaphoreType.DMA((7,)), pltpu.SemaphoreType.REGULAR((3,))]
         + [pltpu.SemaphoreType.DMA((2,))],
         compiler_params=pltpu.CompilerParams(
             collective_id=0, has_side_effects=True, vmem_limit_bytes=60 * 2**20

time: 66.2 us -> 65.2 us (0.985)
  Pallas kernels: 64.5 us -> 63.4 us
    pallas_call x1, Pallas kernels: 62.5 us -> 61.4 us  [shards(): pl.pallas_call(kernel, name='key_projection', out_shape=shapes, in_specs=...]
where the time goes in v5:
time: 65.2 us; the launch traced here: 64.1 us
  Pallas kernels  63.4 us (97%)
    pallas_call x1, Pallas kernels, shards(): pl.pallas_call(kernel, name='key_projection', out_shape=shapes, in_specs=...  61.4 us
    pallas_call x1, Pallas kernels, shards(): pl.pallas_call(place, name='place_results', out_shape=shapes, in_specs=[h...  2.06 us

profile of v5, /device:TPU:1, one launch (start us, length us, event | category | flops | bytes accessed | tf_op | source)
XLA Modules:
  0.0 64.1 jit_solution(1408083397837734206)
XLA Ops:
  0.6 61.4 %key_projection.1 = (bf16[128,512]{1,0:T(8,128)(2,1)}, bf16[128,4096]{1,0:T(8,128)(2,1)}, f32[4,512]{1,0:T(4,128)}) custom-call(bf16[128,4096]{1,0:T(8,128)(2,1)} %tok_hbm.1, f32[1,4096]{1,0:T(1,128)} %bitcast.1, bf16[64,512]{1,0:T(8,128)(2,1)} %w_hbm.1, bf16[128,512]{1,0:T(8,128)(2,1)} %kg_hbm.1), custom_call_target="tpu_custom_call" | custom-call | tf_op jit(solution)/shard_map/key_projection/pallas_call | solution.py:376
  62.0 2.1 %place_results.1 = (bf16[128,512]{1,0:T(8,128)(2,1)}, bf16[128,4096]{1,0:T(8,128)(2,1)}, f32[4,512]{1,0:T(4,128)}) custom-call(bf16[128,512]{1,0:T(8,128)(2,1)} %get-tuple-element.6.keys_in, bf16[128,4096]{1,0:T(8,128)(2,1)} %get-tuple-element.7.ig_in, f32[4,512]{1,0:T(4,128)} %get-tuple-element.8.wg_in), custom_call_target="tpu_custom_call" | custom-call | tf_op jit(solution)/shard_map/place_results/pallas_call | solution.py:414
